TPU v7x, 32 devices: a whole 2x2x4 slice. The times are simulated.
32 devices in a mesh: pipe: 4 (over x, core), dp: 8 (over z, y).
Axes of the slice: x: 2, y: 2, z: 4, core: 2. Of those that a mesh axis runs over, the one named last changes fastest.
Arguments:
- series: bfloat16 [32, 336, 512], P(('pipe', 'dp')), may hold values from -6 to 6
- groups: int32 [32], P(('pipe', 'dp')), may hold values from 0 to 2
- cotangent: bfloat16 [32, 512, 512], P(('pipe', 'dp')), may hold values from -6 to 6
- embed_weight: float32 [624, 512], P(None, 'dp'), may hold values from -0.4375 to 0.4375
- embed_bias: float32 [3, 512], P(None, 'dp'), may hold values from -3 to 3
- qkv_weight: float32 [4, 1536, 512], P('pipe', 'dp'), may hold values from -0.25 to 0.25
- out_weight: float32 [4, 512, 512], P('pipe', 'dp'), may hold values from -2 to 2
- up_weight: float32 [4, 2048, 512], P('pipe', 'dp'), may hold values from -0.25 to 0.25
- down_weight: float32 [4, 512, 2048], P('pipe', 'dp'), may hold values from -0.125 to 0.125
- gains: float32 [4, 1024], P('pipe', 'dp'), may hold values from 0.25 to 1.75
- biases: float32 [4, 5120], P('pipe', 'dp'), may hold values from -2 to 2
Outputs:
- block_output: bfloat16 [32, 512, 512], P(('pipe', 'dp'))
- series_grad: float32 [32, 336, 512], P(('pipe', 'dp'))
- embed_weight_grad: float32 [624, 512], P(None, ('pipe', 'dp'))
- embed_bias_grad: float32 [3, 512], P(None, ('pipe', 'dp'))
- qkv_grad: float32 [4, 1536, 512], P('pipe', 'dp')
- out_grad: float32 [4, 512, 512], P('pipe', 'dp')
- up_grad: float32 [4, 2048, 512], P('pipe', 'dp')
- down_grad: float32 [4, 512, 2048], P('pipe', 'dp')
- gains_grad: float32 [4, 1024], P('pipe', 'dp')
- biases_grad: float32 [4, 5120], P('pipe', 'dp')
All inputs are finite; a program needn't handle non-finite values.
Results may differ from a plain program's by a relative error of at most 0.019.
The roundings to bfloat16 on the way count: a program that leaves them out, or rounds other values in their place, can miss the bound.
Values may be sent and summed in bfloat16 or wider, within the bound.
A program may use at most 384 MiB of HBM per device.

v0:
```python
from functools import partial
import math

import jax
import jax.numpy as jnp
from jax import lax
from jax.experimental import pallas as pl
from jax.experimental.pallas import tpu as pltpu
from jax.sharding import PartitionSpec as P

HEAD = 64
L1 = 96
L2 = 192
L3 = 336
GROUPS = 3


NORM_EPS = 1e-05


MESH = pl.DeviceIdType.MESH
LANES = 128
ZS = 4
SECT = 4
EMB = 3


class Place:
    def __init__(self, dps):
        self.bs = bs = dps // ZS
        pipe = lax.axis_index("pipe")
        dp = lax.axis_index("dp")
        self.pipe, self.dp = pipe, dp
        self.x, self.c = x, c = lax.div(pipe, 2), lax.rem(pipe, 2)
        self.z, self.b = z, b = lax.div(dp, bs), lax.rem(dp, bs)
        self.block = c * 2 + x
        self.other_block = c * 2 + 1 - x
        self.x_peer = ((1 - x) * 2 + c, dp)
        self.core_peer = (x * 2 + 1 - c, dp)
        self.pipes = [lax.rem(pipe + k, SECT) for k in range(SECT)]
        self.blocks = [self.block_of(other) for other in self.pipes]
        self.zs = [lax.rem(z + k, ZS) for k in range(ZS)]
        self.bees = [lax.rem(b + k, bs) for k in range(bs)]
        self.z_peers = [(pipe, other * bs + b) for other in self.zs]
        self.b_peers = [(pipe, z * bs + other) for other in self.bees]

    def block_of(self, pipe):
        return lax.rem(pipe, 2) * 2 + lax.div(pipe, 2)

    def pipe_at(self, step):
        return self.pipes[step % SECT]

    def z_at(self, step):
        return self.zs[step % ZS]

    def b_at(self, step):
        return self.bees[step % self.bs]

    def z_peer(self, step):
        return self.z_peers[step % ZS]

    def b_peer(self, step):
        return self.b_peers[step % self.bs]

    def greet(self):
        barrier = pltpu.get_barrier_semaphore()
        peers = [(self.pipe_at(k), self.dp) for k in range(1, SECT)]
        peers += [self.z_peer(k) for k in range(1, ZS)]
        peers += [self.b_peer(k) for k in range(1, self.bs)]
        for peer in peers:
            pl.semaphore_signal(barrier, inc=1, device_id=peer, device_id_type=MESH)

    def met(self):
        pl.semaphore_wait(pltpu.get_barrier_semaphore(), SECT + ZS + self.bs - 3)


def remote(src, dst, send, recv, peer):
    return pltpu.make_async_remote_copy(
        src_ref=src, dst_ref=dst, send_sem=send, recv_sem=recv, device_id=peer, device_id_type=MESH
    )


FORWARD_START = (
    (0, 3, 0),
    (0, 0, 0),
    (0, 2, 0),
    (1, 3, 0),
    (1, 0, 0),
    (0, 1, 0),
    (2, 3, 0),
    (2, 0, 0),
    (0, 0, 1),
    (1, 1, 0),
    (1, 2, 0),
    (3, 3, 0),
    (0, 2, 1),
    (1, 0, 1),
    (2, 1, 0),
    (4, 3, 0),
    (3, 0, 0),
    ("embed",),
    (4, 0, 0),
)
FORWARD_PERIOD = (
    ("mix",),
    (0, 1, 1),
    (2, 0, 1),
    ("mix",),
    ("attend",),
    (3, 1, 0),
    ("attend",),
    (2, 2, 0),
    ("attend",),
    (0, 0, 2),
    (4, 1, 0),
    ("attend",),
    ("project",),
    (1, 1, 1),
    ("up",),
    (1, 2, 1),
    (0, 2, 2),
    (3, 2, 0),
    ("up",),
    (1, 0, 2),
    ("up",),
    (2, 1, 1),
    (3, 0, 1),
    (4, 2, 0),
    ("up",),
    ("down",),
    (4, 0, 1),
    ("down",),
)
BACKWARD_PERIOD = (
    ("norm2",),
    (1, 0, -1),
    ("down",),
    ("down",),
    ("gelu",),
    ("gelu",),
    (2, 1, -1),
    (0, 2, 0),
    ("up",),
    ("normed",),
    (2, 0, -1),
    ("norm1",),
    (4, 1, -2),
    (4, 2, -2),
    (1, 2, 0),
    (3, 1, -1),
    (0, 1, 0),
    ("attend",),
    ("attend",),
    ("attend",),
    ("attend",),
    (3, 2, -1),
    (1, 1, 0),
    (4, 0, -2),
    (3, 0, -1),
    ("mix",),
    ("mix",),
    (0, 0, 0),
    ("input",),
    (2, 2, 0),
)
BACKWARD_END = (
    ("embed",),
    (1, 0, 3),
    (2, 1, 3),
    (2, 0, 3),
    (4, 1, 2),
    (4, 2, 2),
    (3, 1, 3),
    (0, 3, 0),
    (3, 2, 3),
    (4, 0, 2),
    (1, 3, 0),
    (3, 0, 3),
    (2, 3, 0),
    (3, 3, 0),
    (4, 1, 3),
    (4, 2, 3),
    (4, 0, 3),
    (4, 3, 0),
)


def copies_start(copies):
    for copy in copies:
        copy.start()


def copies_begin(copies):
    for copy in copies:
        copy.start(priority=1)


def copies_wait(copies):
    for copy in copies:
        copy.wait()


class Spread:
    def __init__(self, at, out, send, recv, half=ZS // 2):
        self.at, self.out, self.send, self.recv = at, out, send, recv
        nb = at.bs - 1
        self.slot_z = 0
        self.slot_b1 = ZS - 1
        self.slot_x1 = self.slot_b1 + nb
        self.slot_x2 = self.slot_x1 + 1
        self.slot_b2 = self.slot_x2 + 1
        self.slot_c = self.slot_b2 + nb
        self.half = half

    @staticmethod
    def slots(bs):
        return ZS - 1 + 2 * (bs - 1) + 3

    def copy(self, region, slot, peer):
        return remote(region, region, self.send.at[slot], self.recv.at[slot], peer)

    def copies(self, stage, back):
        at, out, half = self.at, self.out, self.half
        rest = pl.ds(half, ZS - half)
        x_block = at.other_block if back else at.block
        if stage == 0:
            return [
                self.copy(
                    out.at[at.block, at.z_at(ZS - k) if back else at.z, at.b],
                    self.slot_z + k - 1,
                    at.z_peer(k),
                )
                for k in range(1, ZS)
            ]
        if stage == 3:
            core = 1 - at.c if back else at.c
            return [self.copy(out.at[pl.ds(core * 2, 2)], self.slot_c, at.core_peer)]
        copies = []
        for k in range(1, at.bs):
            b = at.b_at(at.bs - k) if back else at.b
            if stage == 1:
                region, slot = out.at[at.block, pl.ds(0, half), b], self.slot_b1
            else:
                region, slot = out.at[pl.ds(at.c * 2, 2), rest, b], self.slot_b2
            copies.append(self.copy(region, slot + k - 1, at.b_peer(k)))
        if stage == 1:
            region, slot = out.at[x_block, rest, at.b], self.slot_x1
        else:
            region, slot = out.at[x_block, pl.ds(0, half)], self.slot_x2
        copies.append(self.copy(region, slot, at.x_peer))
        return copies

    def start(self, stage):
        copies_start(self.copies(stage, False))

    def land(self, stage):
        for copy in self.copies(stage, True):
            copy.wait_recv()
        for copy in self.copies(stage, False):
            copy.wait_send()

    def move(self, stage):
        self.land(stage)
        self.start(stage + 1)


class SpreadCross(Spread):
    @staticmethod
    def slots(bs):
        return 2 * bs + 2 * ZS - 1

    def copies(self, stage, back):
        at, out = self.at, self.out
        rows = out.shape[-2]
        cut = rows // 32 * 16
        some, rest = pl.ds(0, cut), pl.ds(cut, rows - cut)
        core = 1 - at.c if back else at.c
        if stage == 3:
            return [self.copy(out.at[pl.ds(core * 2, 2)], 2 * at.bs + 2 * ZS - 2, at.core_peer)]
        both = pl.ds(at.c * 2, 2)
        x_block = at.other_block if back else at.block
        copies = []
        if stage == 1:
            for k in range(1, ZS):
                z = at.z_at(ZS - k) if back else at.z
                copies.append(self.copy(out.at[both, z, at.b, some], at.bs + k - 1, at.z_peer(k)))
                slot = at.bs + ZS + k - 2
                copies.append(self.copy(out.at[at.block, z, :, rest], slot, at.z_peer(k)))
            return copies
        base = 0 if stage == 0 else at.bs + 2 * ZS - 2
        for k in range(1, at.bs):
            b = at.b_at(at.bs - k) if back else at.b
            region = out.at[at.block, at.z, b, rest] if stage == 0 else out.at[both, :, b, some]
            copies.append(self.copy(region, base + k, at.b_peer(k)))
        if stage == 0:
            region = out.at[x_block, at.z, at.b, some]
        else:
            region = out.at[x_block, :, :, rest]
        copies.append(self.copy(region, base, at.x_peer))
        return copies


class Fold:
    def __init__(self, at, grads, total, landing, bufs, final, send, recv, credit, half):
        self.at, self.grads, self.total = at, grads, total
        self.landing, self.bufs, self.final = landing, bufs, final
        self.send, self.recv, self.credit = send, recv, credit
        self.half = half
        nb = at.bs - 1
        self.slot_x1 = 1
        self.slot_b1 = 2
        self.slot_x2 = 2 + nb
        self.slot_b2 = 3 + nb
        self.slot_z = 3 + 2 * nb

    @staticmethod
    def slots(bs):
        return 3 + 2 * (bs - 1) + ZS - 1

    @staticmethod
    def buffers(bs, rows, half):
        nb = max(bs - 1, 1)
        rest = ZS - half
        return [
            (half, bs, rows, LANES),
            (nb, 2, rest, rows, LANES),
            (rest, rows, LANES),
            (nb, half, rows, LANES),
            (ZS - 1, rows, LANES),
        ]

    def core_parts(self):
        other = self.grads.at[pl.ds((1 - self.at.c) * 2, 2)]
        return [(other, self.landing, 0, self.at.core_peer, self.at.core_peer)]

    def parts(self, stage):
        at, half, total, bufs = self.at, self.half, self.total, self.bufs
        if stage == 0:
            return self.core_parts()
        if stage == 3:
            return [
                (
                    total.at[at.x, at.z_at(k), at.b],
                    bufs[4].at[k - 1],
                    self.slot_z + k - 1,
                    at.z_peer(k),
                    at.z_peer(ZS - k),
                )
                for k in range(1, ZS)
            ]
        rest = pl.ds(half, ZS - half)
        found = []
        for k in range(1, at.bs):
            if stage == 1:
                src, buf, slot = total.at[:, rest, at.b_at(k)], bufs[1], self.slot_b1
            else:
                src, buf, slot = total.at[at.x, pl.ds(0, half), at.b_at(k)], bufs[3], self.slot_b2
            found.append((src, buf.at[k - 1], slot + k - 1, at.b_peer(k), at.b_peer(at.bs - k)))
        if stage == 1:
            src, buf, slot = total.at[1 - at.x, pl.ds(0, half)], bufs[0], self.slot_x1
        else:
            src, buf, slot = total.at[1 - at.x, rest, at.b], bufs[2], self.slot_x2
        found.append((src, buf, slot, at.x_peer, at.x_peer))
        return found

    def start(self, stage, again):
        for src, buf, slot, to, _ in self.parts(stage):
            if again is not False:

                @pl.when(again)
                def _():
                    pl.semaphore_wait(self.credit.at[slot], 1)

            remote(src, buf, self.send.at[slot], self.recv.at[slot], to).start()

    def land(self, stage, more):
        parts = self.parts(stage)
        for src, buf, slot, to, _ in parts:
            remote(src, buf, self.send.at[slot], self.recv.at[slot], to).wait()
        self.add(stage)
        if more is not False:

            @pl.when(more)
            def _():
                for _, _, slot, _, origin in parts:
                    pl.semaphore_signal(
                        self.credit.at[slot], inc=1, device_id=origin, device_id_type=MESH
                    )

    def add_core(self):
        at, bs, total = self.at, self.at.bs, self.total

        @pl.loop(0, 2 * ZS * bs)
        def _(i):
            z, b = i // bs % ZS, i % bs
            x = i // (ZS * bs)
            total[x, z, b] = self.grads[at.c * 2 + x, z, b] + self.landing[x, z, b]

    def add(self, stage):
        at, half, bs = self.at, self.half, self.at.bs
        total, bufs = self.total, self.bufs
        rest = ZS - half
        if stage == 0:
            self.add_core()
        elif stage == 1:

            @pl.loop(0, half * bs)
            def _(i):
                z, b = i // bs, i % bs
                total[at.x, z, b] = total[at.x, z, b] + bufs[0][z, b]

            @pl.loop(0, 2 * rest)
            def _(i):
                x, z = i // rest, i % rest
                for k in range(bs - 1):
                    total[x, half + z, at.b] = total[x, half + z, at.b] + bufs[1][k, x, z]

        elif stage == 2:

            @pl.loop(0, rest)
            def _(z):
                total[at.x, half + z, at.b] = total[at.x, half + z, at.b] + bufs[2][z]

            @pl.loop(0, half)
            def _(z):
                for k in range(bs - 1):
                    total[at.x, z, at.b] = total[at.x, z, at.b] + bufs[3][k, z]

        else:
            self.finish([bufs[4][k] for k in range(ZS - 1)])

    def finish(self, pieces):
        at = self.at
        done = self.total[at.x, at.z, at.b].astype(jnp.float32)
        for piece in pieces:
            done = done + piece.astype(jnp.float32)
        self.final[...] = done.astype(self.final.dtype)

    def move(self, stage, again, more):
        self.land(stage, more)
        self.start(stage + 1, again)


class FoldCross(Fold):
    @staticmethod
    def slots(bs):
        return 2 * bs + 2 * ZS - 1

    @staticmethod
    def buffers(bs, rows, half):
        nb = max(bs - 1, 1)
        cut = rows // 32 * 16
        rest = rows - cut
        return [
            (nb, 2, ZS, cut, LANES),
            (ZS, bs, rest, LANES),
            (ZS - 1, 2, cut, LANES),
            (ZS - 1, bs, rest, LANES),
            (cut, LANES),
            (nb, rest, LANES),
        ]

    def cuts(self):
        rows = self.total.shape[-2]
        cut = rows // 32 * 16
        return pl.ds(0, cut), pl.ds(cut, rows - cut)

    def parts(self, stage):
        at, total, bufs = self.at, self.total, self.bufs
        if stage == 0:
            return self.core_parts()
        some, rest = self.cuts()
        found = []
        if stage == 2:
            for k in range(1, ZS):
                pair = (at.z_peer(k), at.z_peer(ZS - k))
                z = at.z_at(k)
                found.append((total.at[:, z, at.b, some], bufs[2].at[k - 1], at.bs + k, *pair))
                slot = at.bs + ZS + k - 1
                found.append((total.at[at.x, z, :, rest], bufs[3].at[k - 1], slot, *pair))
            return found
        base = 1 if stage == 1 else at.bs + 2 * ZS - 1
        for k in range(1, at.bs):
            pair = (at.b_peer(k), at.b_peer(at.bs - k))
            if stage == 1:
                src, buf = total.at[:, :, at.b_at(k), some], bufs[0].at[k - 1]
            else:
                src, buf = total.at[at.x, at.z, at.b_at(k), rest], bufs[5].at[k - 1]
            found.append((src, buf, base + k, *pair))
        if stage == 1:
            src, buf = total.at[1 - at.x, :, :, rest], bufs[1]
        else:
            src, buf = total.at[1 - at.x, at.z, at.b, some], bufs[4]
        found.append((src, buf, base, at.x_peer, at.x_peer))
        return found

    def add(self, stage):
        at, bs = self.at, self.at.bs
        total, bufs = self.total, self.bufs
        some, rest = self.cuts()
        if stage == 0:
            self.add_core()
        elif stage == 1:

            @pl.loop(0, 2 * ZS)
            def _(i):
                x, z = i // ZS, i % ZS
                for k in range(bs - 1):
                    total[x, z, at.b, some] = total[x, z, at.b, some] + bufs[0][k, x, z]

            @pl.loop(0, ZS * bs)
            def _(i):
                z, b = i // bs, i % bs
                total[at.x, z, b, rest] = total[at.x, z, b, rest] + bufs[1][z, b]

        elif stage == 2:
            for x in range(2):
                for k in range(ZS - 1):
                    total[x, at.z, at.b, some] = total[x, at.z, at.b, some] + bufs[2][k, x]

            @pl.loop(0, bs)
            def _(b):
                for k in range(ZS - 1):
                    total[at.x, at.z, b, rest] = total[at.x, at.z, b, rest] + bufs[3][k, b]

        else:
            total[at.x, at.z, at.b, some] = total[at.x, at.z, at.b, some] + bufs[4][...]
            for k in range(bs - 1):
                total[at.x, at.z, at.b, rest] = total[at.x, at.z, at.b, rest] + bufs[5][k]
            self.final[...] = total[at.x, at.z, at.b]


HALF = 256
WIDE = 512
QKV_TILE = 768
VEC_ROWS = 16


STEP = 64


def by_rows(fn, *arrays, step=STEP):
    parts = [
        fn(*[array[at : at + step] for array in arrays])
        for at in range(0, arrays[0].shape[0], step)
    ]
    if isinstance(parts[0], tuple):
        return tuple(jnp.concatenate(part, axis=0) for part in zip(*parts))
    return jnp.concatenate(parts, axis=0)


def dot_nt(a, b):
    return lax.dot_general(a, b, (((1,), (1,)), ((), ())), preferred_element_type=jnp.float32)


def dot_nn(a, b):
    return lax.dot_general(a, b, (((1,), (0,)), ((), ())), preferred_element_type=jnp.float32)


def dot_tn(a, b):
    return lax.dot_general(a, b, (((0,), (0,)), ((), ())), preferred_element_type=jnp.float32)


def aligned(index, unit):
    return pl.multiple_of(index, unit)


def rows_of(ref, bs, first, count, start, rows, blocks=range(SECT)):
    parts = []
    for i in range(count):
        d = first + i
        place = (d // bs, d % bs)
        parts.append(
            jnp.concatenate(
                [ref[(lb,) + place + (pl.ds(start, rows), slice(None))] for lb in blocks], axis=1
            )
        )
    return parts[0] if count == 1 else jnp.concatenate(parts, axis=0)


def put_rows(ref, bs, first, count, start, rows, value, block=0):
    value = value.astype(ref.dtype)
    for i in range(count):
        d = first + i
        place = (d // bs, d % bs)
        for lane in range(value.shape[1] // LANES):
            ref[(block + lane,) + place + (pl.ds(start, rows), slice(None))] = value[
                i * rows : (i + 1) * rows, lane * LANES : (lane + 1) * LANES
            ]


def vector_pieces(dps):
    n_gains, n_biases = 2 * WIDE // dps, 10 * WIDE // dps
    starts = [(0, 0), (0, 2), (1, 0), (1, 2), (2, 0), (2, 1), (2, 2), (2, 3), (3, 0), (3, 2)]
    pieces = []
    for d in range(dps):
        at = 0
        while at < n_gains + n_biases:
            if at < n_gains:
                index = d * n_gains + at
                row, column = (1, 3)[index // WIDE], WIDE + index % WIDE
                left = n_gains - at
            else:
                index = d * n_biases + at - n_gains
                row, part = starts[index // WIDE]
                column = part * WIDE + index % WIDE
                left = n_gains + n_biases - at
            size = min(left, LANES - at % LANES, LANES - column % LANES)
            pieces.append((d, at // LANES, at % LANES, row, column, size))
            at += size
    return pieces


def read_vectors(ref, table, bs, start, block):
    tiles = {}
    for d, row, lane, to_row, to_lane, size in vector_pieces(ZS * bs):
        if d not in tiles:
            tile = ref[block, d // bs, d % bs, start : start + VEC_ROWS, :]
            tiles[d] = tile.astype(jnp.float32)
        table[to_row : to_row + 1, to_lane : to_lane + size] = tiles[d][
            row : row + 1, lane : lane + size
        ]


def rows_tile(lines):
    row_id = lax.broadcasted_iota(jnp.int32, (VEC_ROWS, LANES), 0)
    tile = jnp.zeros((VEC_ROWS, LANES), jnp.float32)
    for row, pieces in enumerate(lines):
        have = sum(piece.shape[1] for piece in pieces)
        if have < LANES:
            pieces = pieces + [jnp.zeros((1, LANES - have), jnp.float32)]
        line = pieces[0] if len(pieces) == 1 else jnp.concatenate(pieces, axis=1)
        tile = jnp.where(row_id == row, line, tile)
    return tile


def vector_tile(table, dps, place):
    lines = []
    for d, row, lane, to_row, to_lane, size in vector_pieces(dps):
        if d == place:
            if row == len(lines):
                lines.append([])
            lines[row].append(table[to_row : to_row + 1, to_lane : to_lane + size])
    return rows_tile(lines)


def fold_rows(x):
    total = x[:8]
    for at in range(8, x.shape[0], 8):
        total = total + x[at : at + 8]
    return total


def normalize(x):
    mean = jnp.mean(x, axis=1, keepdims=True)
    centred = x - mean
    scale = lax.rsqrt(jnp.mean(centred * centred, axis=1, keepdims=True) + NORM_EPS)
    return centred * scale, jnp.broadcast_to(scale, (x.shape[0], LANES))


def normalize_back(unit, scale, grad, gain):
    inner = grad * gain
    first = jnp.mean(inner, axis=1, keepdims=True)
    second = jnp.mean(inner * unit, axis=1, keepdims=True)
    out = jnp.concatenate([scale] * (WIDE // LANES), axis=1) * (inner - first - unit * second)
    return out, fold_rows(out), fold_rows(grad * unit), fold_rows(grad)


def gelu_pair(u):
    below = 0.5 + 0.5 * lax.erf(u * math.sqrt(0.5))
    bell = jnp.exp2((-0.5 * math.log2(math.e)) * (u * u))
    return u * below, below + u * (bell * (1.0 / math.sqrt(2.0 * math.pi)))


def head_masks(scale):
    lane = lax.broadcasted_iota(jnp.int32, (1, LANES), 1)
    first = jnp.where(lane < HEAD, scale, 0.0).astype(jnp.bfloat16)
    second = jnp.where(lane < HEAD, 0.0, scale).astype(jnp.bfloat16)
    return first, second


class Sizes:
    def __init__(self, dps):
        self.dps, self.bs = dps, dps // ZS
        self.qkv, self.out, self.up, self.down = (
            3 * WIDE // dps,
            WIDE // dps,
            4 * WIDE // dps,
            WIDE // dps,
        )
        self.lookback = -(-6 * WIDE // (SECT * dps) // VEC_ROWS) * VEC_ROWS
        self.emb = self.lookback + VEC_ROWS
        self.dense = self.out + self.up
        self.wide = 4 * self.down


def qkv_rows(size, w, tile):
    count = QKV_TILE // size.qkv
    return rows_of(w, size.bs, tile * count, count, 0, size.qkv)


def out_rows(size, w):
    return rows_of(w, size.bs, 0, size.dps, 0, size.out)


def up_rows(size, w, tile):
    count = HALF // size.up
    return rows_of(w, size.bs, tile * count, count, size.out, size.up)


def forward_mix(size, w, table, h, mixed, piece):
    columns = slice(piece * QKV_TILE, (piece + 1) * QKV_TILE)
    shift = table[0:1, columns]
    out = dot_nt(h[...], qkv_rows(size, w, piece))
    mixed[:, columns] = by_rows(lambda part: (part + shift).astype(mixed.dtype), out)


def softmax_columns(scores):
    parts = [scores[at : at + STEP] for at in range(0, scores.shape[0], STEP)]
    top = parts[0]
    for part in parts[1:]:
        top = jnp.maximum(top, part)
    top = jnp.max(top, axis=0, keepdims=True)
    parts = [jnp.exp(part - top) for part in parts]
    total = parts[0]
    for part in parts[1:]:
        total = total + part
    scale = 1.0 / jnp.sum(total, axis=0, keepdims=True)
    return jnp.concatenate([(part * scale).astype(jnp.bfloat16) for part in parts], axis=0)


def forward_attend(mixed, probs, attended, pair):
    lane = pair * LANES
    key_rows = mixed[:, WIDE + lane : WIDE + lane + LANES]
    values = mixed[:, 2 * WIDE + lane : 2 * WIDE + lane + LANES].T

    for part in range(2):
        rows = slice(part * HALF, (part + 1) * HALF)
        queries = mixed[rows, lane : lane + LANES]
        joined = []
        for head, mask in enumerate(head_masks(1.0 / math.sqrt(HEAD))):
            weights = softmax_columns(dot_nt(key_rows, queries * mask))
            probs[2 * pair + head, :, rows] = weights
            joined.append(dot_nn(values[head * HEAD : (head + 1) * HEAD], weights))
        joined = jnp.concatenate(joined, axis=0).T
        attended[rows, lane : lane + LANES] = joined.astype(attended.dtype)


def forward_project(size, w, table, h, attended, first, scale, normed):
    out = dot_nt(attended[...], out_rows(size, w))
    for part in range(WIDE // STEP):
        rows = slice(part * STEP, (part + 1) * STEP)
        total = h[rows, :].astype(jnp.float32) + (out[rows] + table[1:2, 0:WIDE])
        unit, scale[rows, :] = normalize(total)
        first[rows, :] = unit
        normed[rows, :] = (
            unit * table[1:2, WIDE : 2 * WIDE] + table[1:2, 2 * WIDE : 3 * WIDE]
        ).astype(normed.dtype)


def forward_up(size, w, table, normed, slope, hidden, piece):
    for j in (2 * piece, 2 * piece + 1):
        columns = slice(j * HALF, (j + 1) * HALF)
        shift = table[2:3, columns]
        upper = dot_nt(normed[...], up_rows(size, w, j))
        for part in range(WIDE // STEP):
            rows = slice(part * STEP, (part + 1) * STEP)
            value, grad = gelu_pair(upper[rows] + shift)
            hidden[rows, columns] = value.astype(hidden.dtype)
            slope[rows, columns] = grad.astype(slope.dtype)


def forward_down(size, w, table, normed, hidden, second, scale, h, piece):
    columns = slice(piece * HALF, (piece + 1) * HALF)
    count = size.dps // 2
    matrix = jnp.concatenate(
        [
            rows_of(w, size.bs, piece * count, count, j * size.down, size.down)
            for j in range(4)
        ],
        axis=1,
    )
    out = dot_nt(hidden[...], matrix)
    shift = table[3:4, columns]
    for part in range(WIDE // STEP):
        rows = slice(part * STEP, (part + 1) * STEP)
        second[rows, columns] = normed[rows, columns].astype(jnp.float32) + (out[rows] + shift)
    if piece == 1:
        for part in range(WIDE // STEP):
            rows = slice(part * STEP, (part + 1) * STEP)
            unit, scale[rows, :] = normalize(second[rows, :])
            second[rows, :] = unit
            h[rows, :] = (
                unit * table[3:4, WIDE : 2 * WIDE] + table[3:4, 2 * WIDE : 3 * WIDE]
            ).astype(h.dtype)


def backward_norm_two(table, dtable, dy, second, scale, dnormed, dlow, dlow_t):
    dtable[...] = jnp.zeros_like(dtable)
    sums = [jnp.zeros((8, WIDE), jnp.float32)] * 3
    for part in range(WIDE // STEP):
        rows = slice(part * STEP, (part + 1) * STEP)
        grad, *found = normalize_back(
            second[rows, :],
            scale[rows, :],
            dy[rows, :].astype(jnp.float32),
            table[3:4, WIDE : 2 * WIDE],
        )
        dnormed[rows, :] = grad
        dlow[rows, :] = grad.astype(dlow.dtype)
        sums = [total + new for total, new in zip(sums, found)]
    for i, total in enumerate(sums):
        dtable[3:4, i * WIDE : (i + 1) * WIDE] = jnp.sum(total, axis=0, keepdims=True)
    dlow_t[...] = dlow[...].T


def backward_down(size, grads, hidden, dlow_t, piece):
    @pl.loop(2 * piece, 2 * piece + 2)
    def _(i):
        start = aligned(i * size.down, 16)
        for half in range(2):
            columns = pl.ds(aligned(i * WIDE, WIDE) + half * HALF, HALF)
            value = dot_nn(dlow_t[...], hidden[:, columns])
            put_rows(grads, size.bs, 0, size.dps, start, size.down, value, 2 * half)


def backward_gelu(size, w, dtable, slope, dlow, dup, piece):
    @pl.loop(2 * piece, 2 * piece + 2)
    def _(i):
        start = aligned(i * size.down, 16)
        for half in range(2):
            columns = pl.ds(aligned(i * WIDE, WIDE) + half * HALF, HALF)
            blocks = (2 * half, 2 * half + 1)
            matrix = rows_of(w, size.bs, 0, size.dps, start, size.down, blocks)
            dhidden = dot_nn(dlow[...], matrix)
            total = jnp.zeros((8, HALF), jnp.float32)
            for part in range(WIDE // STEP):
                rows = slice(part * STEP, (part + 1) * STEP)
                dupper = dhidden[rows] * slope[rows, columns].astype(jnp.float32)
                total = total + fold_rows(dupper)
                dup[rows, columns] = dupper.astype(dup.dtype)
            dtable[2:3, columns] = jnp.sum(total, axis=0, keepdims=True)


def backward_up(size, grads, normed, dup):
    count = HALF // size.up

    @pl.loop(0, 4)
    def _(i):
        for half in range(2):
            columns = pl.ds(aligned(i * WIDE, WIDE) + half * HALF, HALF)
            value = dot_tn(dup[:, columns], normed[...])
            first = (2 * i + half) * count
            put_rows(grads, size.bs, first, count, size.out, size.up, value)


def backward_normed(size, w, dnormed, dup):
    for half in range(2):
        columns = slice(half * HALF, (half + 1) * HALF)
        blocks = (2 * half, 2 * half + 1)
        matrix = rows_of(w, size.bs, 0, size.dps, size.out, size.up, blocks)
        out = dot_nn(dup[...], matrix)
        for part in range(WIDE // STEP):
            rows = slice(part * STEP, (part + 1) * STEP)
            dnormed[rows, columns] = dnormed[rows, columns] + out[rows]


def backward_norm_one(
    size, w, table, grads, dtable, first, scale, attended, dnormed, dlow, dlow_t, delta
):
    sums = [jnp.zeros((8, WIDE), jnp.float32)] * 3
    for part in range(WIDE // STEP):
        rows = slice(part * STEP, (part + 1) * STEP)
        grad, *found = normalize_back(
            first[rows, :], scale[rows, :], dnormed[rows, :], table[1:2, WIDE : 2 * WIDE]
        )
        dnormed[rows, :] = grad
        dlow[rows, :] = grad.astype(dlow.dtype)
        sums = [total + new for total, new in zip(sums, found)]
    for i, total in enumerate(sums):
        dtable[1:2, i * WIDE : (i + 1) * WIDE] = jnp.sum(total, axis=0, keepdims=True)
    dlow_t[...] = dlow[...].T
    for block in (0, 2):
        columns = slice(block * LANES, (block + 2) * LANES)
        value = dot_nn(dlow_t[...], attended[:, columns])
        put_rows(grads, size.bs, 0, size.dps, 0, size.out, value, block)
    grad = dot_nn(dlow[...], out_rows(size, w)).astype(dlow.dtype)
    dlow[...] = grad
    product = grad.astype(jnp.float32) * attended[...].astype(jnp.float32)
    high = product.astype(jnp.bfloat16)
    rest = (product - high.astype(jnp.float32)).astype(jnp.bfloat16)
    head = lax.broadcasted_iota(jnp.int32, delta.shape, 0)
    lane = lax.broadcasted_iota(jnp.int32, delta.shape, 1)
    inside = (lane >= head * HEAD) & (lane < (head + 1) * HEAD)
    inside = jnp.where(inside, 1.0, 0.0).astype(jnp.bfloat16)
    delta[...] = dot_nt(inside, high) + dot_nt(inside, rest)


def backward_attend(mixed, probs, delta, dtable, dlow, dmixed, pair):
    scale = 1.0 / math.sqrt(HEAD)
    lane = pair * LANES
    columns = slice(lane, lane + LANES)
    key_columns = slice(WIDE + lane, WIDE + lane + LANES)
    value_columns = slice(2 * WIDE + lane, 2 * WIDE + lane + LANES)
    keys_t = mixed[:, key_columns].T
    values = mixed[:, value_columns]
    dkeys = jnp.zeros((WIDE, LANES), jnp.float32)
    dvalues = jnp.zeros((WIDE, LANES), jnp.float32)
    for part in range(2):
        rows = slice(part * HALF, (part + 1) * HALF)
        queries = mixed[rows, columns]
        grad_out = dlow[rows, columns]
        dqueries = []
        for head in range(2):
            query = queries * head_masks(scale)[head]
            grad = grad_out * head_masks(1.0)[head]
            at = 2 * pair + head
            weights = probs[at, :, rows]
            less = delta[at : at + 1, rows]
            dprobs = dot_nt(values, grad)
            dscores = by_rows(
                lambda p, dp: (p.astype(jnp.float32) * (dp - less)).astype(jnp.bfloat16),
                weights,
                dprobs,
            )
            dvalues = dvalues + dot_nn(weights, grad)
            dkeys = dkeys + dot_nn(dscores, query)
            dqueries.append(dot_nn(keys_t[head * HEAD : (head + 1) * HEAD], dscores))
        dquery = jnp.concatenate(dqueries, axis=0).T * scale
        dtable[0:1, columns] += jnp.sum(dquery, axis=0, keepdims=True)
        dmixed[rows, columns] = dquery.astype(dmixed.dtype)
    dmixed[:, key_columns] = dkeys.astype(dmixed.dtype)
    dmixed[:, value_columns] = dvalues.astype(dmixed.dtype)
    dtable[0:1, value_columns] = jnp.sum(dvalues, axis=0, keepdims=True)


def backward_mix(size, grads, h, dmixed, piece):
    count = QKV_TILE // size.qkv
    grad = dmixed[:, piece * QKV_TILE : (piece + 1) * QKV_TILE]
    put_rows(grads, size.bs, piece * count, count, 0, size.qkv, dot_tn(grad, h[...]))


def backward_input(size, w, dnormed, dmixed, dy):
    for half in range(2):
        columns = slice(half * HALF, (half + 1) * HALF)
        blocks = (2 * half, 2 * half + 1)
        matrix = rows_of(w, size.bs, 0, size.dps, 0, size.qkv, blocks)
        out = dot_nn(dmixed[...], matrix)
        for part in range(WIDE // STEP):
            rows = slice(part * STEP, (part + 1) * STEP)
            dy[rows, columns] = (dnormed[rows, columns] + out[rows]).astype(dy.dtype)


WINDOW = 384


def group_rows(group):
    rows = lax.broadcasted_iota(jnp.int32, (16, LANES), 0)
    return jnp.where(rows == group, 1.0, 0.0).astype(jnp.bfloat16)


def pack_mix(piece, qkv):
    for lb in range(SECT):
        piece[lb] = qkv[:, lb * LANES : (lb + 1) * LANES].astype(piece.dtype)


def pack_up(piece, out, up):
    rows = out.shape[0]
    for lb in range(SECT):
        lanes = slice(lb * LANES, (lb + 1) * LANES)
        piece[lb, :rows] = out[:, lanes].astype(piece.dtype)
        piece[lb, rows:] = up[:, lanes].astype(piece.dtype)


def pack_down(piece, down):
    rows = down.shape[0]
    for lb in range(SECT):
        for j in range(4):
            start = j * WIDE + lb * LANES
            piece[lb, j * rows : (j + 1) * rows] = down[:, start : start + LANES].astype(piece.dtype)


def pack_embedding(piece, weight, shift, gains, biases, square, block):
    n = weight.shape[0]
    square[...] = jnp.zeros_like(square)
    square[:GROUPS, :n] = shift[...]

    def ending(part, width):
        return jnp.concatenate([jnp.zeros((n, width - part.shape[1]), part.dtype), part], axis=1)

    third = ending(weight[:, L1 + L2 :], 3 * LANES)
    second = ending(weight[:, L1 : L1 + L2], 2 * LANES)
    blocks = [third[:, :LANES] + square[...].T[:n]]
    blocks += [third[:, LANES : 2 * LANES], third[:, 2 * LANES :]]
    blocks += [second[:, :LANES], second[:, LANES:], ending(weight[:, :L1], LANES)]
    rows = piece.shape[1] - VEC_ROWS
    if SECT * rows > 6 * n:
        blocks.append(jnp.zeros((SECT * rows - 6 * n, LANES), jnp.float32))
    flat = jnp.concatenate(blocks, axis=0).astype(piece.dtype)
    for lb in range(SECT):
        piece[lb, :rows] = flat[lb * rows : (lb + 1) * rows]
    line = jnp.concatenate([gains[...], biases[...]], axis=1)
    lines = [[line[:, at : at + LANES]] for at in range(0, line.shape[1], LANES)]
    piece[block, rows:] = rows_tile(lines).astype(piece.dtype)


def expand(series, group, x):
    empty = jnp.zeros((WINDOW - series.shape[0], series.shape[1]), series.dtype)
    x[:, :WINDOW] = jnp.concatenate([empty, series[...]], axis=0).T
    lane = lax.broadcasted_iota(jnp.int32, (x.shape[0], LANES), 1)
    x[:, WINDOW:] = jnp.where(lane == group, 1.0, 0.0).astype(x.dtype)


def embed(size, emb, pick, x, wsel, h):
    n = WIDE // size.dps
    flat = []
    for d in range(size.dps):
        place = (d // size.bs, d % size.bs, slice(0, size.lookback), slice(None))
        flat.append(jnp.concatenate([emb[(lb,) + place] for lb in range(SECT)], axis=0))
    blocks = [
        jnp.concatenate([rows[j * n : (j + 1) * n] for rows in flat], axis=0) for j in range(6)
    ]
    long, middle, short = (pick[g : g + 1, :] for g in (2, 1, 0))
    wide = jnp.concatenate(
        [
            blocks[0] * long,
            blocks[1] * long + blocks[3] * middle,
            blocks[2] * long + blocks[4] * middle + blocks[5] * short,
        ],
        axis=1,
    )
    wsel[...] = wide.T
    h[...] = dot_nt(x[...], jnp.concatenate([wide, blocks[0]], axis=1)).astype(h.dtype)


def embed_back(size, pick, x, wsel, dh, tables, grads, series_grad):
    history = series_grad.shape[0]
    series_grad[...] = dot_nt(wsel[...], dh[...])[WINDOW - history :]
    sums = dot_tn(dh[...], x[...])
    long, middle, short = (pick[g : g + 1, :].astype(jnp.float32) for g in (2, 1, 0))
    parts = [sums[:, i * LANES : (i + 1) * LANES] for i in range(4)]
    parts = [
        parts[0] * long + parts[3],
        parts[1] * long,
        parts[2] * long,
        parts[1] * middle,
        parts[2] * middle,
        parts[2] * short,
    ]
    rows = WIDE // (SECT * size.dps)
    spare = size.lookback - 6 * rows
    for pipe in range(SECT):
        block = (pipe % 2) * 2 + pipe // 2
        for dp in range(size.dps):
            start = (pipe * size.dps + dp) * rows
            pieces = [part[start : start + rows] for part in parts]
            if spare:
                pieces.append(jnp.zeros((spare, LANES), jnp.float32))
            pieces.append(vector_tile(tables.at[pipe], size.dps, dp))
            piece = jnp.concatenate(pieces, axis=0)
            grads[block, dp // size.bs, dp % size.bs] = piece.astype(grads.dtype)


def saved_shapes():
    low, wide = jnp.bfloat16, jnp.float32
    return [
        ((WIDE, WIDE), low),
        ((WIDE, 3 * WIDE), low),
        ((2 * SECT, WIDE, WIDE), low),
        ((WIDE, WIDE), low),
        ((WIDE, WIDE), wide),
        ((WIDE, WIDE), low),
        ((WIDE, 4 * WIDE), low),
        ((WIDE, 4 * WIDE), low),
        ((WIDE, WIDE), wide),
        ((SECT, 4 * WIDE), wide),
        ((WIDE, LANES), wide),
        ((WIDE, LANES), wide),
    ]


def chunk_shape(size, rows):
    return (SECT, ZS, size.bs, rows, LANES)


HALVES = (2, 2, 2, 2)
CROSS = (2,)


def follow(plan, section, act, compute):
    seen = {}
    for step in plan:
        if len(step) == 1:
            piece = seen.get(step[0], 0)
            seen[step[0]] = piece + 1
            compute(step[0], piece)
            continue
        op, kind, offset = step
        where = section + offset
        if isinstance(where, int):
            if 0 <= where < SECT:
                act(op, kind, where)
        elif offset == 0:
            act(op, kind, where)
        else:
            inside = where < SECT if offset > 0 else where >= 0

            @pl.when(inside)
            def _():
                act(op, kind, where)


def forward_kernel(dps, groups, *refs):
    size = Sizes(dps)
    given, refs = refs[:9], refs[9:]
    out, copies_out, wsel, x, refs = refs[0], refs[1:4], refs[4], refs[5], refs[6:]
    kept, local, refs = refs[:12], refs[12:24], refs[24:]
    wholes, refs = refs[:4], refs[4:]
    pieces, held, refs = refs[:4], refs[4:13], refs[13:]
    emb_rows, pick, refs = refs[0], refs[1], refs[2:]
    given_sem, out_sem, kept_sem, own_sem, p_send, p_recv, send, recv = refs
    h, mixed, probs, attended, first, normed, slope, hidden, second, table, scale_1, scale_2 = local
    at = Place(dps)

    own = [
        pltpu.make_async_copy(
            pieces[kind].at[at.block],
            wholes[kind].at[at.pipe, at.block, at.z, at.b]
            if kind < EMB
            else wholes[kind].at[at.block, at.z, at.b],
            own_sem.at[kind],
        )
        for kind in range(4)
    ]
    def split(kind, back):
        copies = []
        for k in range(1, SECT):
            if back:
                region = wholes[kind].at[at.pipe_at(SECT - k), at.block, at.z, at.b]
                src = region
            else:
                block = at.blocks[k]
                region = wholes[kind].at[at.pipe, block, at.z, at.b]
                src = pieces[kind].at[block]
            sems = p_send.at[kind, k - 1], p_recv.at[kind, k - 1]
            copies.append(remote(src, region, *sems, (at.pipe_at(k), at.dp)))
        return copies

    def chunk(kind, section):
        if kind == EMB:
            return Spread(at, wholes[kind], send.at[3 * SECT], recv.at[3 * SECT])
        number = 3 * section + kind
        sort = SpreadCross if kind in CROSS else Spread
        return sort(at, wholes[kind].at[section], send.at[number], recv.at[number], HALVES[kind])

    def keep(kind, section):
        src, dst = wholes[kind].at[section], copies_out[kind].at[section]
        return pltpu.make_async_copy(src, dst, out_sem.at[kind, section])

    arrived = []

    def act(op, kind, section):
        if op == 0:
            if kind not in arrived:
                arrived.append(kind)
                own[kind].wait()
                if kind == EMB:
                    chunk(kind, section).start(0)
                    return
                for copy in split(kind, True):
                    copy.wait_recv()
                for copy in split(kind, False):
                    copy.wait_send()
                if kind == 0:
                    copies_start(split(1, False))
                    copies_start(split(2, False))
            chunk(kind, section).start(0)
        elif op < 4:
            chunk(kind, section).move(op - 1)
            if op == 1 and kind == EMB:
                gets[0].wait()
                expand(series, groups[0], x)
        else:
            chunk(kind, section).land(3)
            if kind != EMB:
                keep(kind, section).start(priority=1)

    def saves(section, early):
        which = (1, 2, 3, 4, 5, 9, 10) if early else (6, 7, 8, 11)
        return [
            pltpu.make_async_copy(local[i], kept[i].at[section], kept_sem.at[i]) for i in which
        ]

    series, embed_weight, embed_bias, qkv, out_w, up_w, down_w, gains, biases = held
    gets = copies_of(zip(given, held), given_sem)
    for i in (3, 7, 8, 1, 2, 4, 5, 6, 0):
        gets[i].start(priority=1)
    pick[...] = group_rows(groups[0])
    at.greet()
    gets[3].wait()
    pack_mix(pieces[0], qkv)
    own[0].start(priority=1)
    at.met()
    copies_start(split(0, False))
    copies_wait(gets[1:3] + gets[7:9])
    pack_embedding(
        pieces[EMB], embed_weight, embed_bias, gains, biases, emb_rows, at.block
    )
    own[EMB].start(priority=1)
    copies_wait(gets[4:7])
    pack_up(pieces[1], out_w, up_w)
    own[1].start(priority=1)
    pack_down(pieces[2], down_w)
    own[2].start(priority=1)
    table[...] = jnp.zeros_like(table)

    def before(name, piece):
        embed(size, wholes[EMB], pick, x, wsel, h)

    follow(FORWARD_START, 0, act, before)

    @pl.loop(0, SECT)
    def _(section):
        att, up, down = (ref.at[section] for ref in wholes[:3])
        keep_h = pltpu.make_async_copy(h, kept[0].at[section], kept_sem.at[0])

        def compute(name, piece):
            if name == "mix":
                if piece == 0:

                    @pl.when(section > 0)
                    def _():
                        copies_wait(saves(section - 1, True))

                    keep_h.start(priority=1)
                    block = section % 2 * 2 + section // 2
                    read_vectors(wholes[EMB], table, size.bs, size.lookback, block)
                forward_mix(size, att, table, h, mixed, piece)
            elif name == "attend":
                forward_attend(mixed, probs, attended, piece)
            elif name == "project":
                forward_project(size, up, table, h, attended, first, scale_1, normed)
                copies_begin(saves(section, True))
            elif name == "up":
                if piece == 0:

                    @pl.when(section > 0)
                    def _():
                        copies_wait(saves(section - 1, False))

                forward_up(size, up, table, normed, slope, hidden, piece)
            else:
                if piece == 0:
                    keep_h.wait()
                forward_down(size, down, table, normed, hidden, second, scale_2, h, piece)
                if piece == 1:
                    copies_begin(saves(section, False))

        follow(FORWARD_PERIOD, section, act, compute)

    out[...] = h[...]
    copies_wait(saves(SECT - 1, True))
    copies_wait(saves(SECT - 1, False))
    for kind in range(3):
        copies_wait([keep(kind, section) for section in range(SECT)])


def copies_of(pairs, sems):
    return [pltpu.make_async_copy(src, dst, sems.at[i]) for i, (src, dst) in enumerate(pairs)]


def forward_all(groups, given, dps):
    size = Sizes(dps)
    low, wide = jnp.bfloat16, jnp.float32
    shapes = saved_shapes()
    rows = (size.qkv, size.dense, size.wide, size.emb)
    chunks = [chunk_shape(size, count) for count in rows]
    anywhere = pl.BlockSpec(memory_space=pl.ANY)
    inside = pl.BlockSpec(memory_space=pltpu.VMEM)
    outs = [((WIDE, WIDE), low)]
    outs += [((SECT,) + shape, low) for shape in chunks[:3]]
    outs += [((WINDOW, WIDE), low), ((WIDE, WIDE), low)]
    outs += [((SECT,) + shape, dtype) for shape, dtype in shapes]
    scratch = shapes + [((SECT,) + shape, low) for shape in chunks[:3]] + [(chunks[3], low)]
    scratch += [((SECT, count, LANES), low) for count in rows]
    scratch += [(array.shape, array.dtype) for array in given]
    scratch += [((LANES, LANES), wide), ((16, LANES), low)]
    slots = max(Spread.slots(size.bs), SpreadCross.slots(size.bs))
    dma = pltpu.SemaphoreType.DMA
    return pl.pallas_call(
        partial(forward_kernel, dps),
        out_shape=[jax.ShapeDtypeStruct(shape, dtype) for shape, dtype in outs],
        in_specs=[pl.BlockSpec(memory_space=pltpu.SMEM)] + [anywhere] * len(given),
        out_specs=[inside] + [anywhere] * 3 + [inside] * 2 + [anywhere] * len(shapes),
        scratch_shapes=[pltpu.VMEM(shape, dtype) for shape, dtype in scratch]
        + [
            dma((len(given),)),
            dma((3, SECT)),
            dma((len(shapes),)),
            dma((4,)),
            dma((3, SECT - 1)),
            dma((3, SECT - 1)),
            dma((1 + 3 * SECT, slots)),
            dma((1 + 3 * SECT, slots)),
        ],
        compiler_params=pltpu.CompilerParams(
            collective_id=0, has_side_effects=True, vmem_limit_bytes=60 * 1024 * 1024
        ),
        name="gather_forward",
    )(groups, *given)


FETCHES = {
    ("norm2", 0): (("second", "scale_2"), ("second", "scale_2")),
    ("down", 0): (("hidden",), ()),
    ("down", 1): ((), ("hidden",)),
    ("gelu", 0): (("slope", 2), ()),
    ("gelu", 1): ((), ("slope", 2)),
    ("up", 0): (("normed",), ("normed",)),
    ("normed", 0): ((1,), ()),
    ("norm1", 0): (("first", "scale_1", "attended"), ("first", "scale_1", "attended", 1)),
    ("attend", 0): (("mixed", "probs"), ()),
    ("attend", 3): ((), ("mixed", "probs")),
    ("mix", 0): (("h",), ()),
    ("mix", 1): ((), ("h",)),
    ("input", 0): ((0,), (0,)),
}


def backward_kernel(dps, groups, att, up, down, cotangent, x_in, wsel_in, *refs):
    size = Sizes(dps)
    kept, refs = refs[:12], refs[12:]
    series_grad, outs, refs = refs[0], refs[1:5], refs[5:]
    local, refs = refs[:11], refs[11:]
    tables, w_att, w_up, w_down, dtables, dy, dnormed, dlow, dlow_t, dmixed, dup = refs[:11]
    x, wsel, pick, delta, refs = *refs[11:15], refs[15:]
    kinds = []
    for kind in range(4):
        count = 6 if kind in CROSS else 5
        kinds.append(refs[:4] + (refs[4 : 4 + count],))
        refs = refs[4 + count :]
    w_sem, kept_sem, table_sem, late_sem, out_sem, p_send, p_recv, send, recv, credit = refs
    h, mixed, probs, attended, first, normed, slope, hidden, second, scale_1, scale_2 = local
    at = Place(dps)
    last = SECT - 1

    def weights(kind, section):
        src, dst = ((att, w_att), (up, w_up), (down, w_down))[kind]
        return pltpu.make_async_copy(src.at[section], dst, w_sem.at[kind])

    names = ("h", "mixed", "probs", "attended", "first", "normed", "slope", "hidden", "second")
    names += ("table", "scale_1", "scale_2")
    held = dict(zip(names[:9] + names[10:], local))

    def fetches(section, *wanted):
        found = []
        for name in wanted:
            if isinstance(name, int):
                found.append(weights(name, section))
            else:
                i = names.index(name)
                dst = held[name]
                found.append(pltpu.make_async_copy(kept[i].at[section], dst, kept_sem.at[i]))
        return found

    def chunk(kind, i):
        grads, totals, finals, landing, bufs = kinds[kind]
        sort = FoldCross if kind in CROSS else Fold
        refs = (grads, totals.at[i % 2], landing, bufs, finals.at[i])
        return sort(at, *refs, send.at[kind], recv.at[kind], credit.at[kind], HALVES[kind])

    def hand_over(kind, i):
        landing = outs[kind].at[at.block]
        final = kinds[kind][2].at[i]
        return (
            pltpu.make_async_copy(final, landing, out_sem.at[kind]),
            remote(final, landing, p_send.at[kind, i], p_recv.at[kind, at.pipe], (last - i, at.dp)),
        )

    def act(op, kind, i):
        again, more = (False, False) if kind == EMB else (i > 0, i < last)
        if op == 0:
            chunk(kind, i).start(0, again)
        elif op < 4:
            chunk(kind, i).move(op - 1, again, more)
        else:
            chunk(kind, i).land(3, more)
            if kind == EMB:
                outs[kind][...] = kinds[kind][2][0]
            else:
                here, away = hand_over(kind, i)

                @pl.when(at.pipe == last - i)
                def _():
                    here.start(priority=1)

                @pl.when(at.pipe != last - i)
                def _():
                    away.start()

    at.greet()
    get_tables = pltpu.make_async_copy(kept[9], tables, table_sem)
    late = copies_of(((cotangent, dy), (x_in, x), (wsel_in, wsel)), late_sem)
    copies_begin([late[0], get_tables] + fetches(last, "second", "scale_2", "hidden"))
    copies_begin(fetches(last, "slope", 2, "normed", 1, "first", "scale_1", "attended"))
    copies_begin(fetches(last, "mixed", "probs", "h", 0) + late[1:])
    pick[...] = group_rows(groups[0])
    copies_wait([late[0], get_tables])

    @pl.loop(0, SECT)
    def _(i):
        section = last - i
        table, dtable = tables.at[section], dtables.at[section]

        def compute(name, piece):
            need, free = FETCHES.get((name, piece), ((), ()))
            copies_wait(fetches(section, *need))
            if name == "norm2":
                backward_norm_two(table, dtable, dy, second, scale_2, dnormed, dlow, dlow_t)
                pl.when(i == 0)(at.met)
            elif name == "down":
                backward_down(size, kinds[2][0], hidden, dlow_t, piece)
            elif name == "gelu":
                backward_gelu(size, w_down, dtable, slope, dlow, dup, piece)
            elif name == "up":
                backward_up(size, kinds[1][0], normed, dup)
            elif name == "normed":
                backward_normed(size, w_up, dnormed, dup)
            elif name == "norm1":
                backward_norm_one(
                    size,
                    w_up,
                    table,
                    kinds[1][0],
                    dtable,
                    first,
                    scale_1,
                    attended,
                    dnormed,
                    dlow,
                    dlow_t,
                    delta,
                )
            elif name == "attend":
                backward_attend(mixed, probs, delta, dtable, dlow, dmixed, piece)
            elif name == "mix":
                backward_mix(size, kinds[0][0], h, dmixed, piece)
            else:
                backward_input(size, w_att, dnormed, dmixed, dy)
            if free:

                @pl.when(section > 0)
                def _():
                    copies_begin(fetches(section - 1, *free))

        follow(BACKWARD_PERIOD, i, act, compute)

    def after(name, piece):
        copies_wait(late[1:])
        embed_back(size, pick, x, wsel, dy, dtables, kinds[EMB][0], series_grad)

    follow(BACKWARD_END, 0, act, after)

    for kind in range(3):
        for i in range(SECT):
            here, away = hand_over(kind, i)

            @pl.when(at.pipe == last - i)
            def _():
                here.wait()

            @pl.when(at.pipe != last - i)
            def _():
                away.wait_send()

        for k in range(1, SECT):
            other = at.pipe_at(k)
            landing = outs[kind].at[at.blocks[k]]
            sems = p_send.at[kind, 0], p_recv.at[kind, other]
            remote(landing, landing, *sems, (other, at.dp)).wait_recv()


def backward_all(groups, weights, cotangent, x, wsel, kept, history, dps):
    size = Sizes(dps)
    low, wide = jnp.bfloat16, jnp.float32
    anywhere = pl.BlockSpec(memory_space=pl.ANY)
    inside = pl.BlockSpec(memory_space=pltpu.VMEM)
    shapes = saved_shapes()
    kind_rows = (size.qkv, size.dense, size.wide, size.emb)
    scratch = shapes[:9] + shapes[10:] + [((SECT,) + shapes[9][0], wide)]
    scratch += [(chunk_shape(size, rows), low) for rows in kind_rows[:3]]
    scratch += [
        ((SECT,) + shapes[9][0], wide),
        ((WIDE, WIDE), low),
        ((WIDE, WIDE), wide),
        ((WIDE, WIDE), low),
        ((WIDE, WIDE), low),
        ((WIDE, 3 * WIDE), low),
        ((WIDE, 4 * WIDE), low),
        ((WIDE, WIDE), low),
        ((WINDOW, WIDE), low),
        ((16, LANES), low),
        ((16, WIDE), wide),
    ]
    for kind, rows in enumerate(kind_rows):
        sets, results = (1, 1) if kind == EMB else (2, SECT)
        scratch += [
            (chunk_shape(size, rows), low),
            ((sets, 2, ZS, size.bs, rows, LANES), low),
            ((results, rows, LANES), low),
            ((2, ZS, size.bs, rows, LANES), low),
        ]
        sort = FoldCross if kind in CROSS else Fold
        scratch += [(shape, low) for shape in sort.buffers(size.bs, rows, HALVES[kind])]
    slots = max(Fold.slots(size.bs), FoldCross.slots(size.bs))
    dma = pltpu.SemaphoreType.DMA
    return pl.pallas_call(
        partial(backward_kernel, dps),
        out_shape=[jax.ShapeDtypeStruct((history, WIDE), wide)]
        + [jax.ShapeDtypeStruct((SECT, rows, LANES), low) for rows in kind_rows[:3]]
        + [jax.ShapeDtypeStruct((size.emb, LANES), low)],
        in_specs=[pl.BlockSpec(memory_space=pltpu.SMEM)] + [anywhere] * (6 + len(kept)),
        out_specs=[inside] + [anywhere] * 3 + [inside],
        scratch_shapes=[pltpu.VMEM(shape, dtype) for shape, dtype in scratch]
        + [
            dma((3,)),
            dma((12,)),
            dma(()),
            dma((3,)),
            dma((3,)),
            dma((3, SECT)),
            dma((3, SECT)),
            dma((4, slots)),
            dma((4, slots)),
            pltpu.SemaphoreType.REGULAR((4, slots)),
        ],
        compiler_params=pltpu.CompilerParams(
            collective_id=1, has_side_effects=True, vmem_limit_bytes=60 * 1024 * 1024
        ),
        name="backward_fold",
    )(groups, *weights, cotangent, x, wsel, *kept)


def finish_kernel(dps, n_gains, n_biases, *refs):
    size = Sizes(dps)
    given, refs = refs[:6], refs[6:]
    block_out, series_out, embed_w, embed_b, qkv, out, up_out, down_out, gains, biases = refs[:10]
    att, up, down, emb, sems = refs[10:]
    copies = copies_of(zip(given, (att, up, down, emb, block_out, series_out)), sems)
    copies_start(copies)
    copies_wait(copies[:4])
    for lb in range(SECT):
        lanes = slice(lb * LANES, (lb + 1) * LANES)
        qkv[:, lanes] = att[lb].astype(jnp.float32)
        out[:, lanes] = up[lb, : size.out].astype(jnp.float32)
        up_out[:, lanes] = up[lb, size.out :].astype(jnp.float32)
        for j in range(4):
            rows = slice(j * size.down, (j + 1) * size.down)
            start = j * WIDE + lb * LANES
            down_out[:, start : start + LANES] = down[lb, rows].astype(jnp.float32)
    vectors = emb[size.lookback :].astype(jnp.float32)
    count = -(-(n_gains + n_biases) // LANES)
    flat = jnp.concatenate([vectors[row : row + 1] for row in range(count)], axis=1)
    gains[...] = flat[:, :n_gains]
    biases[...] = flat[:, n_gains : n_gains + n_biases]
    rows = WIDE // (SECT * dps)
    packed = emb[: size.lookback].astype(jnp.float32)
    packed = [packed[i * rows : (i + 1) * rows] for i in range(6)]
    square = jnp.concatenate([packed[0], jnp.zeros((LANES - rows, LANES), jnp.float32)], axis=0)
    embed_b[...] = square.T[:GROUPS, :rows]
    packed = jnp.concatenate(packed, axis=1)
    ends = ((6 * LANES, L1), (5 * LANES, L2), (3 * LANES, L3))
    embed_w[...] = jnp.concatenate([packed[:, end - span : end] for end, span in ends], axis=1)
    copies_wait(copies[4:])


def finish_all(sums, block, series, n_gains, n_biases, dps):
    size = Sizes(dps)
    wide = jnp.float32
    columns = WIDE // (SECT * dps)
    outs = [
        (block.shape, block.dtype),
        (series.shape, wide),
        ((columns, L1 + L2 + L3), wide),
        ((GROUPS, columns), wide),
        ((size.qkv, WIDE), wide),
        ((size.out, WIDE), wide),
        ((size.up, WIDE), wide),
        ((size.down, 4 * WIDE), wide),
        ((1, n_gains), wide),
        ((1, n_biases), wide),
    ]
    anywhere = pl.BlockSpec(memory_space=pl.ANY)
    inside = pl.BlockSpec(memory_space=pltpu.VMEM)
    return pl.pallas_call(
        partial(finish_kernel, dps, n_gains, n_biases),
        out_shape=[jax.ShapeDtypeStruct(shape, dtype) for shape, dtype in outs],
        in_specs=[anywhere] * 6,
        out_specs=[inside] * 10,
        scratch_shapes=[pltpu.VMEM(array.shape, array.dtype) for array in sums]
        + [pltpu.SemaphoreType.DMA((6,))],
        compiler_params=pltpu.CompilerParams(vmem_limit_bytes=60 * 1024 * 1024),
        name="finish",
    )(*sums, block, series)


def per_device(
    series,
    groups,
    cotangent,
    embed_weight,
    embed_bias,
    qkv_weight,
    out_weight,
    up_weight,
    down_weight,
    gains,
    biases,
):
    dps = lax.axis_size("dp")
    given = (
        series[0],
        embed_weight.T,
        embed_bias,
        qkv_weight[0],
        out_weight[0],
        up_weight[0],
        down_weight[0],
        gains,
        biases,
    )
    block_output, att, up, down, wsel, x, *kept = forward_all(groups, given, dps)
    series_grad, *sums = backward_all(
        groups, (att, up, down), cotangent[0], x, wsel, kept, series.shape[1], dps
    )
    outs = finish_all(sums, block_output, series_grad, gains.shape[1], biases.shape[1], dps)
    block_output, series_grad, embed_w, embed_b, qkv, out, up, down, gain_sum, bias_sum = outs
    return (
        block_output[None],
        series_grad[None],
        embed_w.T,
        embed_b,
        qkv[None],
        out[None],
        up[None],
        down[None],
        gain_sum,
        bias_sum,
    )


def solution(mesh):
    return jax.shard_map(
        per_device,
        mesh=mesh,
        in_specs=(
            P(("pipe", "dp"), None, None),
            P(("pipe", "dp")),
            P(("pipe", "dp"), None, None),
            P(None, "dp"),
            P(None, "dp"),
            P("pipe", "dp", None),
            P("pipe", "dp", None),
            P("pipe", "dp", None),
            P("pipe", "dp", None),
            P("pipe", "dp"),
            P("pipe", "dp"),
        ),
        out_specs=(
            P(("pipe", "dp"), None, None),
            P(("pipe", "dp"), None, None),
            P(None, ("pipe", "dp")),
            P(None, ("pipe", "dp")),
            P("pipe", "dp", None),
            P("pipe", "dp", None),
            P("pipe", "dp", None),
            P("pipe", "dp", None),
            P("pipe", "dp"),
            P("pipe", "dp"),
        ),
        check_vma=False,
    )
```

profile of v0, /device:TPU:0, one launch (start us, length us, event | category | flops | bytes accessed | tf_op | source)
XLA Modules:
  0.0 275.5 jit_solution(1854102566952618264)
XLA Ops:
  1.3 132.9 %gather_forward.1 = (bf16[512,512]{1,0:T(8,128)(2,1)}, bf16[4,4,4,2,192,128]{5,4,3,2,1,0:T(8,128)(2,1)}, bf16[4,4,4,2,320,128]{5,4,3,2,1,0:T(8,128)(2,1)}, bf16[...) custom-call(s32[1]{0:T(128)S(6)} %copy.21.groups, ...), custom_call_target="tpu_custom_call" | custom-call | tf_op jit(solution)/shard_map/gather_forward/pallas_call | solution.py:1290
  134.2 137.9 %backward_fold.1 = (f32[336,512]{1,0:T(8,128)}, bf16[4,192,128]{2,1,0:T(8,128)(2,1)}, bf16[4,320,128]{2,1,0:T(8,128)(2,1)}, bf16[4,256,128]{2,1,0:T(8,128)(2,1)}, bf16[112,128]{1,0:T(8,128)(2,1)}) custom-call(s32[1]{0:T(128)S(6)} %copy.21.groups, bf16[4,4,4,2,192,128]{5,4,3,2,1,0:T(8,128)(2,1)} %get-tuple-element.43.att, ...), custom_call_target="tpu_custom_call" | custom-call | tf_op jit(solution)/shard_map/backward_fold/pallas_call | solution.py:1517
  272.2 3.2 %finish.1 = (bf16[512,512]{1,0:T(8,128)(2,1)}, f32[336,512]{1,0:T(8,128)}, f32[16,624]{1,0:T(8,128)}, f32[3,16]{1,0:T(4,128)}, f32[192,512]{1,0:T(8,128)}, /*ind...) custom-call(bf16[4,192,128]{2,1,0:T(8,128)(2,1)} %get-tuple-element.60.refs_, ...), custom_call_target="tpu_custom_call" | custom-call | tf_op jit(solution)/shard_map/finish/pallas_call | solution.py:1595
where the time goes:
time: 276 us
  Pallas kernels  274 us (99%)
    pallas_call x1, Pallas kernels, backward_all(): pl.pallas_call(partial(backward_kernel, dps), out_shape=[jax.ShapeDtypeSt...  138 us
    pallas_call x1, Pallas kernels, forward_all(): pl.pallas_call(partial(forward_kernel, dps), out_shape=[jax.ShapeDtypeStr...  133 us

commit v1 on v0

--- a/solution.py
+++ b/solution.py
@@ -214,10 +214,25 @@
 
     @staticmethod
     def slots(bs):
-        return ZS - 1 + 2 * (bs - 1) + 3
+        return ZS - 1 + 3 * (bs - 1) + 5
 
     def copy(self, region, slot, peer):
         return remote(region, region, self.send.at[slot], self.recv.at[slot], peer)
+
+    def core_regions(self, core):
+        at, out = self.at, self.out
+        some, rest = pl.ds(0, self.half), pl.ds(self.half, ZS - self.half)
+        both = pl.ds(core * 2, 2)
+        late = [out.at[core * 2 + 1 - at.x, some]]
+        late += [out.at[both, rest, at.b_at(k)] for k in range(1, at.bs)]
+        return [out.at[core * 2 + at.x, some], out.at[both, rest, at.b]], late
+
+    def core_copies(self, back, early, late):
+        groups = self.core_regions(1 - self.at.c if back else self.at.c)
+        regions = [(i, region) for i, region in enumerate(groups[0])] if early else []
+        if late:
+            regions += [(2 + i, region) for i, region in enumerate(groups[1])]
+        return [self.copy(region, self.slot_c + i, self.at.core_peer) for i, region in regions]
 
     def copies(self, stage, back):
         at, out, half = self.at, self.out, self.half
@@ -232,9 +247,6 @@
                 )
                 for k in range(1, ZS)
             ]
-        if stage == 3:
-            core = 1 - at.c if back else at.c
-            return [self.copy(out.at[pl.ds(core * 2, 2)], self.slot_c, at.core_peer)]
         copies = []
         for k in range(1, at.bs):
             b = at.b_at(at.bs - k) if back else at.b
@@ -251,12 +263,19 @@
         return copies
 
     def start(self, stage):
-        copies_start(self.copies(stage, False))
+        if stage < 3:
+            copies_start(self.copies(stage, False))
+        if stage >= 2:
+            copies_start(self.core_copies(False, stage == 2, stage == 3))
 
     def land(self, stage):
-        for copy in self.copies(stage, True):
+        if stage < 3:
+            here, away = self.copies(stage, True), self.copies(stage, False)
+        else:
+            here, away = (self.core_copies(back, True, True) for back in (True, False))
+        for copy in here:
             copy.wait_recv()
-        for copy in self.copies(stage, False):
+        for copy in away:
             copy.wait_send()
 
     def move(self, stage):
@@ -267,16 +286,28 @@
 class SpreadCross(Spread):
     @staticmethod
     def slots(bs):
-        return 2 * bs + 2 * ZS - 1
+        return 3 * bs + 2 * ZS
+
+    def __init__(self, *args):
+        super().__init__(*args)
+        self.slot_c = 2 * self.at.bs + 2 * ZS - 2
+
+    def cuts(self):
+        rows = self.out.shape[-2]
+        cut = rows // 32 * 16
+        return pl.ds(0, cut), pl.ds(cut, rows - cut)
+
+    def core_regions(self, core):
+        at, out = self.at, self.out
+        some, rest = self.cuts()
+        both = pl.ds(core * 2, 2)
+        late = [out.at[core * 2 + 1 - at.x, :, :, rest]]
+        late += [out.at[both, :, at.b_at(k), some] for k in range(1, at.bs)]
+        return [out.at[both, :, at.b, some], out.at[core * 2 + at.x, :, :, rest]], late
 
     def copies(self, stage, back):
         at, out = self.at, self.out
-        rows = out.shape[-2]
-        cut = rows // 32 * 16
-        some, rest = pl.ds(0, cut), pl.ds(cut, rows - cut)
-        core = 1 - at.c if back else at.c
-        if stage == 3:
-            return [self.copy(out.at[pl.ds(core * 2, 2)], 2 * at.bs + 2 * ZS - 2, at.core_peer)]
+        some, rest = self.cuts()
         both = pl.ds(at.c * 2, 2)
         x_block = at.other_block if back else at.block
         copies = []

time: 276 us -> 275 us (level)
  no operation moved by 1% of the time
where the time goes in v1:
time: 275 us
  Pallas kernels  273 us (99%)
    pallas_call x1, Pallas kernels, backward_all(): pl.pallas_call(partial(backward_kernel, dps), out_shape=[jax.ShapeDtypeSt...  137 us
    pallas_call x1, Pallas kernels, forward_all(): pl.pallas_call(partial(forward_kernel, dps), out_shape=[jax.ShapeDtypeStr...  133 us

profile of v1, /device:TPU:0, one launch (start us, length us, event | category | flops | bytes accessed | tf_op | source)
XLA Modules:
  0.0 274.7 jit_solution(16650765648126673195)
XLA Ops:
  1.3 133.2 %gather_forward.1 = (bf16[512,512]{1,0:T(8,128)(2,1)}, bf16[4,4,4,2,192,128]{5,4,3,2,1,0:T(8,128)(2,1)}, bf16[4,4,4,2,320,128]{5,4,3,2,1,0:T(8,128)(2,1)}, bf16[...) custom-call(s32[1]{0:T(128)S(6)} %copy.21.groups, ...), custom_call_target="tpu_custom_call" | custom-call | tf_op jit(solution)/shard_map/gather_forward/pallas_call | solution.py:1321
  134.5 136.8 %backward_fold.1 = (f32[336,512]{1,0:T(8,128)}, bf16[4,192,128]{2,1,0:T(8,128)(2,1)}, bf16[4,320,128]{2,1,0:T(8,128)(2,1)}, bf16[4,256,128]{2,1,0:T(8,128)(2,1)}, bf16[112,128]{1,0:T(8,128)(2,1)}) custom-call(s32[1]{0:T(128)S(6)} %copy.21.groups, bf16[4,4,4,2,192,128]{5,4,3,2,1,0:T(8,128)(2,1)} %get-tuple-element.43.att, ...), custom_call_target="tpu_custom_call" | custom-call | tf_op jit(solution)/shard_map/backward_fold/pallas_call | solution.py:1548
  271.3 3.2 %finish.1 = (bf16[512,512]{1,0:T(8,128)(2,1)}, f32[336,512]{1,0:T(8,128)}, f32[16,624]{1,0:T(8,128)}, f32[3,16]{1,0:T(4,128)}, f32[192,512]{1,0:T(8,128)}, /*ind...) custom-call(bf16[4,192,128]{2,1,0:T(8,128)(2,1)} %get-tuple-element.60.refs_, ...), custom_call_target="tpu_custom_call" | custom-call | tf_op jit(solution)/shard_map/finish/pallas_call | solution.py:1626

commit v2 on v0

--- a/solution.py
+++ b/solution.py
@@ -956,7 +956,7 @@
 
 def group_rows(group):
     rows = lax.broadcasted_iota(jnp.int32, (16, LANES), 0)
-    return jnp.where(rows == group, 1.0, 0.0).astype(jnp.bfloat16)
+    return jnp.where(rows == group, 1.0, 0.0)
 
 
 def pack_mix(piece, qkv):
@@ -1020,15 +1020,16 @@
     blocks = [
         jnp.concatenate([rows[j * n : (j + 1) * n] for rows in flat], axis=0) for j in range(6)
     ]
+    parts = [block.astype(jnp.float32) for block in blocks]
     long, middle, short = (pick[g : g + 1, :] for g in (2, 1, 0))
     wide = jnp.concatenate(
         [
-            blocks[0] * long,
-            blocks[1] * long + blocks[3] * middle,
-            blocks[2] * long + blocks[4] * middle + blocks[5] * short,
+            parts[0] * long,
+            parts[1] * long + parts[3] * middle,
+            parts[2] * long + parts[4] * middle + parts[5] * short,
         ],
         axis=1,
-    )
+    ).astype(jnp.bfloat16)
     wsel[...] = wide.T
     h[...] = dot_nt(x[...], jnp.concatenate([wide, blocks[0]], axis=1)).astype(h.dtype)
 
@@ -1037,7 +1038,7 @@
     history = series_grad.shape[0]
     series_grad[...] = dot_nt(wsel[...], dh[...])[WINDOW - history :]
     sums = dot_tn(dh[...], x[...])
-    long, middle, short = (pick[g : g + 1, :].astype(jnp.float32) for g in (2, 1, 0))
+    long, middle, short = (pick[g : g + 1, :] for g in (2, 1, 0))
     parts = [sums[:, i * LANES : (i + 1) * LANES] for i in range(4)]
     parts = [
         parts[0] * long + parts[3],
@@ -1284,7 +1285,7 @@
     scratch = shapes + [((SECT,) + shape, low) for shape in chunks[:3]] + [(chunks[3], low)]
     scratch += [((SECT, count, LANES), low) for count in rows]
     scratch += [(array.shape, array.dtype) for array in given]
-    scratch += [((LANES, LANES), wide), ((16, LANES), low)]
+    scratch += [((LANES, LANES), wide), ((16, LANES), wide)]
     slots = max(Spread.slots(size.bs), SpreadCross.slots(size.bs))
     dma = pltpu.SemaphoreType.DMA
     return pl.pallas_call(
@@ -1499,7 +1500,7 @@
         ((WIDE, 4 * WIDE), low),
         ((WIDE, WIDE), low),
         ((WINDOW, WIDE), low),
-        ((16, LANES), low),
+        ((16, LANES), wide),
         ((16, WIDE), wide),
     ]
     for kind, rows in enumerate(kind_rows):

time: 276 us -> 276 us (level)
  no operation moved by 1% of the time
where the time goes in v2:
time: 276 us; the launch traced here: 275 us
  Pallas kernels  274 us (99%)
    pallas_call x1, Pallas kernels, backward_all(): pl.pallas_call(partial(backward_kernel, dps), out_shape=[jax.ShapeDtypeSt...  138 us
    pallas_call x1, Pallas kernels, forward_all(): pl.pallas_call(partial(forward_kernel, dps), out_shape=[jax.ShapeDtypeStr...  133 us

profile of v2, /device:TPU:0, one launch (start us, length us, event | category | flops | bytes accessed | tf_op | source)
XLA Modules:
  0.0 275.5 jit_solution(5235897613756286949)
XLA Ops:
  1.3 133.0 %gather_forward.1 = (bf16[512,512]{1,0:T(8,128)(2,1)}, bf16[4,4,4,2,192,128]{5,4,3,2,1,0:T(8,128)(2,1)}, bf16[4,4,4,2,320,128]{5,4,3,2,1,0:T(8,128)(2,1)}, bf16[...) custom-call(s32[1]{0:T(128)S(6)} %copy.21.groups, ...), custom_call_target="tpu_custom_call" | custom-call | tf_op jit(solution)/shard_map/gather_forward/pallas_call | solution.py:1291
  134.3 137.9 %backward_fold.1 = (f32[336,512]{1,0:T(8,128)}, bf16[4,192,128]{2,1,0:T(8,128)(2,1)}, bf16[4,320,128]{2,1,0:T(8,128)(2,1)}, bf16[4,256,128]{2,1,0:T(8,128)(2,1)}, bf16[112,128]{1,0:T(8,128)(2,1)}) custom-call(s32[1]{0:T(128)S(6)} %copy.21.groups, bf16[4,4,4,2,192,128]{5,4,3,2,1,0:T(8,128)(2,1)} %get-tuple-element.43.att, ...), custom_call_target="tpu_custom_call" | custom-call | tf_op jit(solution)/shard_map/backward_fold/pallas_call | solution.py:1518
  272.2 3.2 %finish.1 = (bf16[512,512]{1,0:T(8,128)(2,1)}, f32[336,512]{1,0:T(8,128)}, f32[16,624]{1,0:T(8,128)}, f32[3,16]{1,0:T(4,128)}, f32[192,512]{1,0:T(8,128)}, /*ind...) custom-call(bf16[4,192,128]{2,1,0:T(8,128)(2,1)} %get-tuple-element.60.refs_, ...), custom_call_target="tpu_custom_call" | custom-call | tf_op jit(solution)/shard_map/finish/pallas_call | solution.py:1596
